TPU v7x, 32 devices: a whole 2x2x4 slice. The times are simulated.
32 devices in a mesh: dp: 16 (over z, y, x), seq: 2 (over core).
Axes of the slice: x: 2, y: 2, z: 4, core: 2. Of those that a mesh axis runs over, the one named last changes fastest.
Arguments:
- patches: bfloat16 [64, 544, 768], P('dp', 'seq'), may hold values from -6 to 6
- lengths: int32 [64], P('dp'), may hold values from 40 to 529, as said below
- gain_one: float32 [768], replicated, may hold values from 0.5 to 1.5
- shift_one: float32 [768], replicated, may hold values from -2 to 2
- w_query: bfloat16 [768, 768], replicated, may hold values from -0.21875 to 0.21875
- b_query: float32 [768], replicated, may hold values from -2 to 2
- w_key: bfloat16 [768, 768], replicated, may hold values from -0.21875 to 0.21875
- w_value: bfloat16 [768, 768], replicated, may hold values from -0.21875 to 0.21875
- b_value: float32 [768], replicated, may hold values from -2 to 2
- w_out: bfloat16 [768, 768], replicated, may hold values from -1.75 to 1.75
- b_out: float32 [768], replicated, may hold values from -2 to 2
- gain_two: float32 [768], replicated, may hold values from 0.5 to 1.5
- shift_two: float32 [768], replicated, may hold values from -2 to 2
- w_up: bfloat16 [768, 3072], replicated, may hold values from -0.21875 to 0.21875
- b_up: float32 [3072], replicated, may hold values from -2 to 2
- w_down: bfloat16 [3072, 768], replicated, may hold values from -0.109375 to 0.109375
- b_down: float32 [768], replicated, may hold values from -2 to 2
- cotangent: bfloat16 [64, 544, 768], P('dp', 'seq'), may hold values from -6 to 6
Outputs:
- output: bfloat16 [64, 544, 768], P('dp', 'seq')
- grad_patches: bfloat16 [64, 544, 768], P('dp', 'seq')
- grad_gain_one: float32 [768], replicated
- grad_shift_one: float32 [768], replicated
- grad_w_query: float32 [768, 768], replicated
- grad_b_query: float32 [768], replicated
- grad_w_key: float32 [768, 768], replicated
- grad_w_value: float32 [768, 768], replicated
- grad_b_value: float32 [768], replicated
- grad_w_out: float32 [768, 768], replicated
- grad_b_out: float32 [768], replicated
- grad_gain_two: float32 [768], replicated
- grad_shift_two: float32 [768], replicated
- grad_w_up: float32 [768, 3072], replicated
- grad_b_up: float32 [3072], replicated
- grad_w_down: float32 [3072, 768], replicated
- grad_b_down: float32 [768], replicated
Inputs may be any that keep to these rules, and one draw needn't show every extreme that they name: `lengths`: in each aligned block of 4 strips one strip has exactly 529 valid patches; valid patches come first in a strip.
All inputs are finite; a program needn't handle non-finite values.
Results may differ from a plain program's by a relative error of at most 0.012.
Values may be sent and summed in bfloat16 or wider, within the bound.
No kernel may reach another device: no remote copies, remote signals or barrier semaphores. Data moves between devices by JAX's collectives and lax.ppermute only.
A program may use at most 256 MiB of HBM per device.

v0:
```python
import jax
import jax.numpy as jnp
from jax import lax
from jax.sharding import PartitionSpec as P

HEAD_DIM = 64
epsilon = 1e-06


def exact_gelu(values):
    return jax.nn.gelu(values, approximate=False)


def project(left_rows, weight):
    return jnp.dot(left_rows, weight, preferred_element_type=jnp.float32)


def project_back(grad_rows, weight):
    return jnp.einsum("stf,df->std", grad_rows, weight, preferred_element_type=jnp.float32)


def weight_grad(left_rows, grad_rows):
    return jnp.einsum("std,stf->df", left_rows, grad_rows, preferred_element_type=jnp.float32)


def column_sums(grad_rows):
    return jnp.sum(grad_rows.astype(jnp.float32), axis=(0, 1))


def norm_forward(values, gain, shift):
    centre = jnp.mean(values, axis=-1, keepdims=True)
    centred = values - centre
    spread = jnp.mean(centred * centred, axis=-1, keepdims=True)
    rstd_rows = lax.rsqrt(spread + epsilon)
    scaled = centred * rstd_rows
    return ((scaled * gain + shift).astype(jnp.bfloat16), scaled, rstd_rows)


def norm_backward(grad_out, scaled, rstd_rows, gain):
    weighted = grad_out * gain
    mean_grad = jnp.mean(weighted, axis=-1, keepdims=True)
    mean_cross = jnp.mean(weighted * scaled, axis=-1, keepdims=True)
    grad_in = rstd_rows * (weighted - mean_grad - scaled * mean_cross)
    return (grad_in, jnp.sum(grad_out * scaled, axis=(0, 1)), jnp.sum(grad_out, axis=(0, 1)))


def split_heads(block_rows):
    return block_rows.reshape(block_rows.shape[0], block_rows.shape[1] // HEAD_DIM, HEAD_DIM)


def masked_scores(query_heads, key_heads, length):
    score_scale = HEAD_DIM ** (-0.5)
    scores = (
        jnp.einsum("qhd,khd->hqk", query_heads, key_heads, preferred_element_type=jnp.float32)
        * score_scale
    )
    key_valid = lax.iota(jnp.int32, key_heads.shape[0]) < length
    return jnp.where(key_valid[None, None, :], scores, -jnp.inf)


def attend(block_item):
    query_block, key_block, value_block, length = block_item
    value_heads = split_heads(value_block)
    scores = masked_scores(split_heads(query_block), split_heads(key_block), length)
    row_max = jnp.max(scores, axis=-1, keepdims=True)
    exponent = jnp.exp(scores - row_max)
    row_total = jnp.sum(exponent, axis=-1, keepdims=True)
    attn_probs = (exponent / row_total).astype(jnp.bfloat16)
    log_total = (row_max + jnp.log(row_total))[..., 0]
    context_rows = jnp.einsum(
        "hqk,khd->qhd", attn_probs, value_heads, preferred_element_type=jnp.float32
    )
    return (context_rows.reshape(context_rows.shape[0], -1).astype(jnp.bfloat16), log_total)


def attend_back(block_item):
    query_block, key_block, value_block, grad_block, log_total, length = block_item
    score_scale = HEAD_DIM ** (-0.5)
    query_heads = split_heads(query_block)
    key_heads = split_heads(key_block)
    value_heads = split_heads(value_block)
    grad_heads = split_heads(grad_block)
    scores = masked_scores(query_heads, key_heads, length)
    probs_exact = jnp.exp(scores - log_total[:, :, None])
    attn_probs = probs_exact.astype(jnp.bfloat16)
    grad_values = jnp.einsum(
        "hqk,qhd->khd", attn_probs, grad_heads, preferred_element_type=jnp.float32
    )
    grad_probs = jnp.einsum(
        "qhd,khd->hqk", grad_heads, value_heads, preferred_element_type=jnp.float32
    )
    inner = jnp.sum(grad_probs * probs_exact, axis=-1, keepdims=True)
    grad_scores = (probs_exact * (grad_probs - inner)).astype(jnp.bfloat16)
    grad_queries = (
        jnp.einsum("hqk,khd->qhd", grad_scores, key_heads, preferred_element_type=jnp.float32)
        * score_scale
    )
    grad_keys = (
        jnp.einsum("hqk,qhd->khd", grad_scores, query_heads, preferred_element_type=jnp.float32)
        * score_scale
    )
    slots = query_block.shape[0]
    return (
        grad_queries.reshape(slots, -1).astype(jnp.bfloat16),
        grad_keys.reshape(slots, -1).astype(jnp.bfloat16),
        grad_values.reshape(slots, -1).astype(jnp.bfloat16),
    )


def local(
    patches,
    lengths,
    gain_one,
    shift_one,
    w_query,
    b_query,
    w_key,
    w_value,
    b_value,
    w_out,
    b_out,
    gain_two,
    shift_two,
    w_up,
    b_up,
    w_down,
    b_down,
    cotangent,
):
    inputs = patches.astype(jnp.float32)
    normed_one, scaled_one, rstd_one = norm_forward(inputs, gain_one, shift_one)
    queries = (project(normed_one, w_query) + b_query).astype(jnp.bfloat16)
    key_rows = project(normed_one, w_key).astype(jnp.bfloat16)
    value_rows = (project(normed_one, w_value) + b_value).astype(jnp.bfloat16)
    query_whole, key_whole, value_whole = (
        lax.all_to_all(queries, "seq", split_axis=2, concat_axis=1, tiled=True),
        lax.all_to_all(key_rows, "seq", split_axis=2, concat_axis=1, tiled=True),
        lax.all_to_all(value_rows, "seq", split_axis=2, concat_axis=1, tiled=True),
    )
    context_whole, log_totals = lax.map(attend, (query_whole, key_whole, value_whole, lengths))
    context = lax.all_to_all(context_whole, "seq", split_axis=1, concat_axis=2, tiled=True)
    hidden = inputs + project(context, w_out) + b_out
    normed_two, scaled_two, rstd_two = norm_forward(hidden, gain_two, shift_two)
    upper_pre = project(normed_two, w_up) + b_up
    active = exact_gelu(upper_pre).astype(jnp.bfloat16)
    output = (hidden + project(active, w_down) + b_down).astype(jnp.bfloat16)
    grad_y = cotangent.astype(jnp.float32)
    g_down = weight_grad(active, cotangent)
    g_bdown = jnp.sum(grad_y, axis=(0, 1))
    grad_active = project_back(cotangent, w_down)
    unused_value, gelu_pull = jax.vjp(exact_gelu, upper_pre)
    grad_upper = gelu_pull(grad_active)[0].astype(jnp.bfloat16)
    g_up = weight_grad(normed_two, grad_upper)
    g_bup = column_sums(grad_upper)
    grad_normed_two = project_back(grad_upper, w_up)
    grad_from_two, g_gain_two, g_shift_two = norm_backward(
        grad_normed_two, scaled_two, rstd_two, gain_two
    )
    grad_hidden = grad_y + grad_from_two
    grad_attn = grad_hidden.astype(jnp.bfloat16)
    g_out = weight_grad(context, grad_attn)
    g_bout = column_sums(grad_attn)
    grad_context = project_back(grad_attn, w_out).astype(jnp.bfloat16)
    grad_context_whole = lax.all_to_all(
        grad_context, "seq", split_axis=2, concat_axis=1, tiled=True
    )
    grad_q_whole, grad_k_whole, grad_v_whole = lax.map(
        attend_back, (query_whole, key_whole, value_whole, grad_context_whole, log_totals, lengths)
    )
    grad_queries, grad_keys, grad_values = (
        lax.all_to_all(grad_q_whole, "seq", split_axis=1, concat_axis=2, tiled=True),
        lax.all_to_all(grad_k_whole, "seq", split_axis=1, concat_axis=2, tiled=True),
        lax.all_to_all(grad_v_whole, "seq", split_axis=1, concat_axis=2, tiled=True),
    )
    g_query = weight_grad(normed_one, grad_queries)
    g_bquery = column_sums(grad_queries)
    g_key = weight_grad(normed_one, grad_keys)
    g_value = weight_grad(normed_one, grad_values)
    g_bvalue = column_sums(grad_values)
    grad_normed_one = (
        project_back(grad_queries, w_query)
        + project_back(grad_keys, w_key)
        + project_back(grad_values, w_value)
    )
    grad_from_one, g_gain_one, g_shift_one = norm_backward(
        grad_normed_one, scaled_one, rstd_one, gain_one
    )
    grad_patches = (grad_hidden + grad_from_one).astype(jnp.bfloat16)
    (
        g_gain_one,
        g_shift_one,
        g_query,
        g_bquery,
        g_key,
        g_value,
        g_bvalue,
        g_out,
        g_bout,
        g_gain_two,
        g_shift_two,
        g_up,
        g_bup,
        g_down,
        g_bdown,
    ) = lax.psum(
        (
            g_gain_one,
            g_shift_one,
            g_query,
            g_bquery,
            g_key,
            g_value,
            g_bvalue,
            g_out,
            g_bout,
            g_gain_two,
            g_shift_two,
            g_up,
            g_bup,
            g_down,
            g_bdown,
        ),
        ("dp", "seq"),
    )
    return (
        output,
        grad_patches,
        g_gain_one,
        g_shift_one,
        g_query,
        g_bquery,
        g_key,
        g_value,
        g_bvalue,
        g_out,
        g_bout,
        g_gain_two,
        g_shift_two,
        g_up,
        g_bup,
        g_down,
        g_bdown,
    )


def solution(mesh):
    return jax.shard_map(
        local,
        mesh=mesh,
        in_specs=(
            P("dp", "seq", None),
            P("dp"),
            P(),
            P(),
            P(),
            P(),
            P(),
            P(),
            P(),
            P(),
            P(),
            P(),
            P(),
            P(),
            P(),
            P(),
            P(),
            P("dp", "seq", None),
        ),
        out_specs=(
            P("dp", "seq", None),
            P("dp", "seq", None),
            P(),
            P(),
            P(),
            P(),
            P(),
            P(),
            P(),
            P(),
            P(),
            P(),
            P(),
            P(),
            P(),
            P(),
            P(),
        ),
        check_vma=False,
    )
```

profile of v0, /device:TPU:0, one launch (start us, length us, event | category | flops | bytes accessed | tf_op | source)
XLA Modules:
  0.0 909.4 jit_solution(8345375993950918164)
XLA Ops:
  11.3 2.9 add_convert_fusion.4
  14.2 5.1 copy.101
  19.4 5.1 all-to-all-start
  24.5 4.2 add_convert_fusion.3
  28.7 5.1 copy.104
  33.9 4.9 all-to-all-start.1
  38.8 7.2 copy.136
  46.0 2.8 copy.103
  48.8 3.8 copy.110
  52.6 4.2 convolution_convert_fusion.1
  56.8 5.1 copy.107
  62.0 5.5 all-to-all-start.2
  67.4 7.2 copy.137
  74.6 2.8 copy.106
  77.4 3.8 copy.111
  81.3 7.2 copy.138
  88.5 2.8 copy.109
  91.3 3.8 copy.112
  96.6 45.2 %while.26 = (s32[]{:T(128)}, bf16[4,544,384]{1,2,0:T(8,128)(2,1)}, f32[4,6,544]{2,1,0:T(8,128)}, bf16[4,544,384]{1,2,0:T(8,128)(2,1)}, s32[4]{0:T(128)S(1)}, /*i...) while((s32[]{:T(128)}, bf16[4,544,384]{1,2,0:T(8,128)(2,1)}, ...), condition=%wide.region_5.6_spmd, body=%wide.region_2.5_spmd.sunk | while | flops 476071264 | bytes 26508796 | solution.py:140
  104.1 2.3 fusion.122
  141.8 4.7 copy.113
  146.5 6.4 all_to_all.144
  156.7 11.9 %fusion.47 = (u8[272,3072]{1,0:T(8,128)(4,1)S(1)}, u8[272,3072]{1,0:T(8,128)(4,1)S(1)}, f32[4,272,3072]{2,1,0:T(8,128)S(1)}) fusion(f32[3072]{0:T(1024)S(1)} %copy-done.30, bf16[768,3072]{1,0:T(8,128)(2,1)} %param.35, f32[4,272,768]{2,1,0:T(8,128)S(1)} %get-tuple-element.238, f32[768]{0:T(1024)S(1)} %copy-done.44, f32[768]{0:T(1024)S(1)} %copy-done.32, ...), kind=kOutput, calls=%fused_computation.101 | convolution fusion | flops 5183127552 | bytes 23128576 | tf_op jit(solution)/shard_map/dot_general | solution.py:15
  168.6 32.4 %multiply_convert_fusion.1 = (bf16[4,272,3072]{2,1,0:T(8,128)(2,1)}, f32[4,272,3072]{2,1,0:T(8,128)}) fusion(f32[4,272,3072]{2,1,0:T(8,128)S(1)} %get-tuple-element.239, f32[3072]{0:T(1024)S(1)} %copy-done.30, u8[272,3072]{1,0:T(8,128)(4,1)S(1)} %get-tuple-element.166, u8[272,3072]{1,0:T(8,128)(4,1)S(1)} %get-tuple-element.165), kind=kLoop, calls=%fused_computation.46 | loop fusion | flops 237305856 | bytes 35106816 | tf_op jit(solution)/shard_map/convert_element_type | solution.py:145
  201.0 19.9 %convert_reduce_fusion = (f32[3072]{0:T(1024)}, bf16[4,272,3072]{2,1,0:T(8,128)(2,1)}) fusion(f32[4,272,3072]{2,1,0:T(8,128)} %get-tuple-element.227, bf16[4,272,768]{2,1,0:T(8,128)(2,1)} %param.39, bf16[3072,768]{1,0:T(8,128)(2,1)} %param.37, f32[4,272,3072]{2,1,0:T(8,128)} %copy-done.9, f32[3072]{0:T(1024)S(1)} %copy-done.30), kind=kOutput, calls=%fused_computation.44 | convolution fusion | flops 5190644736 | bytes 39837696 | tf_op jit(solution)/shard_map/stf,df->std/dot_general | solution.py:19
  220.9 10.6 %multiply_reduce_fusion.1 = (f32[768]{0:T(1024)}, f32[4,272]{1,0:T(4,128)S(1)}, f32[4,272]{1,0:T(4,128)S(1)}, f32[768]{0:T(1024)}, f32[4,272,768]{2,1,0:T(8,128)S(1)}) fusion(f32[4,272,768]{2,1,0:T(8,128)S(1)} %copy-done.6, f32[4,272]{1,0:T(4,128)S(1)} %add_rsqrt_fusion, f32[4,272]{1,0:T(4,128)S(1)} %broadcast_multiply_fusion.4, f32[768]{0:T(1024)S(1)} %copy-done.32, ...), kind=kOutput, calls=%fused_computation.89 | convolution fusion | flops 5141344256 | bytes 18114560 | tf_op jit(solution)/shard_map/stf,df->std/dot_general | solution.py:19
  235.6 2.7 convolution_convert_fusion
  238.3 3.9 copy.116
  242.3 6.9 all_to_all.145
  249.2 7.0 copy.139
  261.9 104.6 %while.27 = (s32[]{:T(128)}, bf16[4,544,384]{1,2,0:T(8,128)(2,1)}, bf16[4,544,384]{1,2,0:T(8,128)(2,1)}, bf16[4,544,384]{1,2,0:T(8,128)(2,1)}, bf16[4,544,384]{1...) while((s32[]{:T(128)}, bf16[4,544,384]{1,2,0:T(8,128)(2,1)}, ...), condition=%wide.region_12.13_spmd, body=%wide.region_10.12_spmd.sunk | while | flops 1164070272 | bytes 89513552 | solution.py:167
  264.0 4.7 fusion.133
  273.1 5.9 multiply_reduce_fusion.7
  279.1 2.6 multiply_convert_fusion.3
  290.2 4.7 fusion.133
  299.3 5.9 multiply_reduce_fusion.7
  305.2 2.6 multiply_convert_fusion.3
  316.4 4.7 fusion.133
  325.4 5.9 multiply_reduce_fusion.7
  331.4 2.6 multiply_convert_fusion.3
  342.5 4.7 fusion.133
  351.6 5.9 multiply_reduce_fusion.7
  357.6 2.6 multiply_convert_fusion.3
  366.5 4.8 copy.129
  371.3 4.7 all-to-all-start.7
  376.0 5.2 convolution_bitcast_fusion.2
  381.3 12.3 %convolution_bitcast_fusion.1 = f32[768,3072]{1,0:T(8,128)} fusion(bf16[4,272,3072]{2,1,0:T(8,128)(2,1)} %get-tuple-element.243, f32[4,272,768]{2,1,0:T(8,128)S(1)} %copy-done.7, f32[768]{0:T(1024)S(1)} %copy-done.45, f32[768]{0:T(1024)S(1)} %copy-done.33, f32[4,272]{1,0:T(4,128)S(1)} %add_rsqrt_fusion, f32[4,272]{1,0:T(4,128)S(1)} %broadcast_multiply_fusion.4), kind=kOutput, calls=%fused_computation.60 | convolution fusion | flops 5138006016 | bytes 19479040 | tf_op jit(solution)/shard_map/std,stf->df/dot_general | solution.py:23
  393.6 3.0 copy.123
  396.6 4.7 all-to-all-start.5
  404.3 4.7 copy.126
  409.0 4.6 all-to-all-start.6
  420.4 3.6 convolution_bitcast_fusion.5
  423.9 3.6 convolution_bitcast_fusion.4
  427.5 3.6 convolution_bitcast_fusion.3
  431.1 9.1 %convolution_bitcast_fusion = f32[3072,768]{1,0:T(8,128)} fusion(bf16[4,272,3072]{2,1,0:T(8,128)(2,1)S(1)} %bitcast.225, bf16[4,272,768]{2,1,0:T(8,128)(2,1)S(1)} %copy-done.23), kind=kOutput, calls=%fused_computation.59 | convolution fusion | flops 5133828096 | bytes 17793024 | tf_op jit(solution)/shard_map/std,stf->df/dot_general | solution.py:23
  442.3 3.4 fusion.55
  447.7 3.8 fusion.43
  451.6 45.7 %all-reduce = (f32[768]{0:T(1024)}, f32[768]{0:T(1024)}, f32[768]{0:T(1024)}, f32[768]{0:T(1024)}, f32[768]{0:T(1024)}, /*index=5*/f32[768]{0:T(1024)}, f32[768]{0:T(1024)}, f32[3072]{0:T(1024)}, f32[768]{0:T(1024)}) all-reduce(f32[768]{0:T(1024)S(1)} %get-tuple-element.169, ...), channel_id=1, replica_groups=mesh['dp'=16,'seq'=2] {'dp','seq'}, use_global_device_ids=true, to_apply=%region_16.17 | all-reduce | flops 9216 | bytes 73728 | tf_op jit(solution)/shard_map/psum | solution.py:205
  497.4 5.2 fusion.42
  502.6 10.0 %add_convert_fusion.1 = bf16[4,272,768]{2,1,0:T(8,128)(2,1)} fusion(f32[4,272,768]{2,1,0:T(8,128)S(1)} %copy-done.8, bf16[4,272,3072]{2,1,0:T(8,128)(2,1)} %get-tuple-element.226, bf16[3072,768]{1,0:T(8,128)(2,1)} %param.37, f32[768]{0:T(1024)S(1)} %copy-done.48), kind=kOutput, calls=%fused_computation.95 | convolution fusion | flops 5136334848 | bytes 16419840 | tf_op jit(solution)/shard_map/dot_general | solution.py:15
  512.6 366.8 %all-reduce.4.cloned.1.call-done = (f32[768,768]{1,0:T(8,128)}, f32[768,768]{1,0:T(8,128)}, f32[768,768]{1,0:T(8,128)}, f32[768,768]{1,0:T(8,128)}, f32[768,3072]{1,0:T(8,128)}, /*index=5*/f32[3072,768]{1,0:T(8,128)}) async-done(((f32[768,768]{1,0:T(8,128)}, f32[768,768]{1,0:T(8,128)}, f32[768,768]{1,0:T(8,128)}, f32[768,768]{1,0:T(8,128)}, f32[768,3072]{1,0:T(8,128)}, /*index=5*/f32[3072,768]{1,0:T(8,128)}), ...) | async-done | bytes 28311568 | tf_op jit(solution)/shard_map/psum | solution.py:205
  879.4 3.4 copy.181
  889.2 9.3 %copy.185 = f32[768,3072]{1,0:T(8,128)} copy(f32[768,3072]{1,0:T(8,128)} %get-tuple-element.436) | data formatting | bytes 18874368
  898.5 3.7 copy.186
  (263 shorter events, 133.5 us)
Async XLA Ops:
  7.2 4.1 copy-start
  7.2 4.1 copy-start.2
  7.2 4.0 copy-start.41
  7.2 4.0 copy-start.46
  7.2 4.0 copy-start.34
  9.2 43.5 %copy-start.24 = (f32[4,272]{1,0:T(4,128)}, f32[4,272]{1,0:T(4,128)S(1)}, u32[]{:S(2)}) copy-start(f32[4,272]{1,0:T(4,128)S(1)} %broadcast_multiply_fusion.5) | copy-start | bytes 13060
  11.3 41.3 %copy-start.26 = (f32[4,272]{1,0:T(4,128)}, f32[4,272]{1,0:T(4,128)S(1)}, u32[]{:S(2)}) copy-start(f32[4,272]{1,0:T(4,128)S(1)} %add_rsqrt_fusion.1) | copy-start | bytes 13060
  19.4 5.1 copy-start.42
  19.4 14.5 %all-to-all-start = ((bf16[4,272,768]{1,0,2:T(4,128)(2,1)}), bf16[4,272,768]{1,0,2:T(4,128)(2,1)}, u32[]{:S(2)}, u32[]{:S(2)}) async-start(bf16[4,272,768]{1,0,2:T(4,128)(2,1)} %copy.101), calls=%async_computation | async-start | bytes 4718592 | tf_op jit(solution)/shard_map/all_to_all | solution.py:138
  33.9 28.1 %all-to-all-start.1 = ((bf16[4,272,768]{1,0,2:T(4,128)(2,1)}), bf16[4,272,768]{1,0,2:T(4,128)(2,1)}, u32[]{:S(2)}, u32[]{:S(2)}) async-start(bf16[4,272,768]{1,0,2:T(4,128)(2,1)} %copy.104), calls=%async_computation.1 | async-start | bytes 4718592 | tf_op jit(solution)/shard_map/all_to_all | solution.py:136
  62.0 19.3 %all-to-all-start.2 = ((bf16[4,272,768]{1,0,2:T(4,128)(2,1)}), bf16[4,272,768]{1,0,2:T(4,128)(2,1)}, u32[]{:S(2)}, u32[]{:S(2)}) async-start(bf16[4,272,768]{1,0,2:T(4,128)(2,1)} %copy.107), calls=%async_computation.2 | async-start | bytes 4718592 | tf_op jit(solution)/shard_map/all_to_all | solution.py:137
  91.3 5.3 copy-start.49
  153.3 2.6 copy-start.15
  155.9 12.7 %copy-start.5 = (f32[4,272,768]{2,1,0:T(8,128)}, f32[4,272,768]{2,1,0:T(8,128)S(1)}, u32[]{:S(2)}) copy-start(f32[4,272,768]{2,1,0:T(8,128)S(1)} %get-tuple-element.238) | copy-start | bytes 10027012
  168.6 32.4 %copy-start.9 = (f32[4,272,3072]{2,1,0:T(8,128)}, f32[4,272,3072]{2,1,0:T(8,128)S(1)}, u32[]{:S(2)}) copy-start(f32[4,272,3072]{2,1,0:T(8,128)S(1)} %get-tuple-element.239) | copy-start | bytes 40108036
  201.0 19.9 %copy-start.6 = (f32[4,272,768]{2,1,0:T(8,128)S(1)}, f32[4,272,768]{2,1,0:T(8,128)}, u32[]{:S(2)}) copy-start(f32[4,272,768]{2,1,0:T(8,128)} %copy-done.5) | copy-start | bytes 10027012
  220.9 10.6 %copy-start.22 = (bf16[4,272,768]{2,1,0:T(8,128)(2,1)S(1)}, bf16[4,272,768]{2,1,0:T(8,128)(2,1)}, u32[]{:S(2)}) copy-start(bf16[4,272,768]{2,1,0:T(8,128)(2,1)} %param.39) | copy-start | bytes 5013508
  231.5 4.1 copy-start.39
  233.8 1.8 copy-start.10
  257.6 4.3 copy-start.50
  273.1 6.0 slice-start
  273.1 6.0 slice-start.1
  299.2 6.0 slice-start
  299.3 6.0 slice-start.1
  325.4 6.0 slice-start
  325.4 6.0 slice-start.1
  351.6 6.0 slice-start
  351.6 6.0 slice-start.1
  366.5 9.5 %copy-start.16 = (bf16[4,2,34,8,384]{4,3,1,2,0:T(8,128)(2,1)S(1)}, bf16[4,2,34,8,384]{4,3,1,2,0:T(8,128)(2,1)}, u32[]{:S(2)}) copy-start(bf16[4,2,34,8,384]{4,3,1,2,0:T(8,128)(2,1)} %copy-done.15) | copy-start | bytes 5013508
  371.3 25.3 %all-to-all-start.7 = ((bf16[4,544,384]{2,0,1:T(4,128)(2,1)}), bf16[4,544,384]{2,0,1:T(4,128)(2,1)}, u32[]{:S(2)}, u32[]{:S(2)}) async-start(bf16[4,544,384]{2,0,1:T(4,128)(2,1)} %copy.129), calls=%async_computation.7 | async-start | bytes 3342336 | tf_op jit(solution)/shard_map/all_to_all | solution.py:173
  376.0 5.3 copy-start.7
  376.0 5.3 copy-start.33
  376.0 5.3 copy-start.45
  381.3 12.3 %copy-start.11 = (bf16[4,544,384]{1,2,0:T(8,128)(2,1)S(1)}, bf16[4,544,384]{1,2,0:T(8,128)(2,1)}, u32[]{:S(2)}) copy-start(bf16[4,544,384]{1,2,0:T(8,128)(2,1)} %get-tuple-element.111) | copy-start | bytes 5013508
  396.6 12.4 %all-to-all-start.5 = ((bf16[4,544,384]{2,0,1:T(4,128)(2,1)}), bf16[4,544,384]{2,0,1:T(4,128)(2,1)}, u32[]{:S(2)}, u32[]{:S(2)}) async-start(bf16[4,544,384]{2,0,1:T(4,128)(2,1)} %copy.123), calls=%async_computation.5 | async-start | bytes 3342336 | tf_op jit(solution)/shard_map/all_to_all | solution.py:171
  409.0 8.9 all-to-all-start.6
  413.6 465.8 %all-reduce.4.cloned.1.call-start = ((), (), s32[]{:S(2)}) async-start(), calls=%async_computation.8 | async-start | bytes 56623104 | tf_op jit(solution)/shard_map/psum | solution.py:205
  417.8 2.0 copy-start.25
  417.8 2.1 copy-start.27
  417.8 2.1 copy-start.35
  417.9 2.1 copy-start.47
  417.9 2.1 copy-start.3
  417.9 2.5 copy-start.19
  419.9 4.0 copy-start.20
  423.9 3.6 copy-start.17
  423.9 7.2 slice-start.5
  427.5 3.6 slice-start.6
  427.5 3.6 copy-start.23
  442.3 3.5 copy-start.21
  442.3 3.5 copy-start.40
  445.8 1.9 copy-start.18
  447.7 3.9 copy-start.28
  447.7 3.9 copy-start.29
  447.7 3.9 copy-start.31
  447.7 3.9 copy-start.36
  447.7 3.9 copy-start.37
  497.4 5.2 copy-start.8
  497.4 5.2 copy-start.48
  879.4 3.4 copy-start.14
  882.8 2.5 copy-start.13
  885.3 2.5 copy-start.12
  887.8 10.7 %slice-start.2 = ((s8[9437184]{0:T(1024)(128)(4,1)}), s8[4194304]{0:T(1024)(128)(4,1)S(1)}, s32[]{:S(2)}) async-start(s8[9437184]{0:T(1024)(128)(4,1)} %bitcast.211), calls=%async_computation.11 | async-start | bytes 8388608
  889.2 9.3 %slice-start.3 = ((s8[9437184]{0:T(1024)(128)(4,1)}), s8[4194304]{0:T(1024)(128)(4,1)S(1)}, s32[]{:S(2)}) async-start(s8[9437184]{0:T(1024)(128)(4,1)} %bitcast.211), calls=%async_computation.12 | async-start | bytes 8388608
  889.2 9.3 %slice-start.4 = ((s8[9437184]{0:T(1024)(128)(4,1)}), s8[1048576]{0:T(1024)(128)(4,1)S(1)}, s32[]{:S(2)}) async-start(s8[9437184]{0:T(1024)(128)(4,1)} %bitcast.211), calls=%async_computation.13 | async-start | bytes 2097152
  (7 other events, 7.6 us)
Sparse Core Ops, SparseCore 0:
  440.4 438.9 all-reduce.3
where the time goes:
time: 919 us; the launch traced here: 909 us
  waiting for transfers between devices  367 us (40%)
  matrix products  192 us (21%)
  local copies, waits for them, and re-layouts  175 us (19%)
  other arithmetic  72.5 us (8%)
  blocking collectives  59.1 us (6%)
  starting transfers between devices  29.5 us (3%)
  between operations  14.9 us (2%)
    psum x1, waiting for transfers between devices, local(): lax.psum((g_gain_one, g_shift_one, g_query, g_bquery, g_key, g_value, g_b...  367 us
    psum x1, blocking collectives, local(): lax.psum((g_gain_one, g_shift_one, g_query, g_bquery, g_key, g_value, g_b...  45.7 us
    dot_general x6, matrix products, project_back(): jnp.einsum('stf,df->std', grad_rows, weight, preferred_element_type=jnp.f...  42 us
    dot_general x6, matrix products, weight_grad(): jnp.einsum('std,stf->df', left_rows, grad_rows, preferred_element_type=jn...  37.4 us
    dot_general x6, matrix products, project(): return jnp.dot(left_rows, weight, preferred_element_type=jnp.float32)  34.9 us
    convert_element_type x1, other arithmetic, local(): active = exact_gelu(upper_pre).astype(jnp.bfloat16)  32.4 us
    dynamic_slice x36, local copies, waits for them, and re-layouts, local(): lax.map(attend, (query_whole, key_whole, value_whole, lengths))  32.2 us
    unnamed x118, local copies, waits for them, and re-layouts  28 us
  transfers between devices with their start and end apart: 7, of which 1 were waited for; matrix products, arithmetic and copies ran while one was open for 11% of the time, Pallas kernels for 0%

commit v1 on v0

--- a/solution.py
+++ b/solution.py
@@ -203,24 +203,27 @@
         g_down,
         g_bdown,
     ) = lax.psum(
-        (
-            g_gain_one,
-            g_shift_one,
-            g_query,
-            g_bquery,
-            g_key,
-            g_value,
-            g_bvalue,
-            g_out,
-            g_bout,
-            g_gain_two,
-            g_shift_two,
-            g_up,
-            g_bup,
-            g_down,
-            g_bdown,
+        lax.psum(
+            (
+                g_gain_one,
+                g_shift_one,
+                g_query,
+                g_bquery,
+                g_key,
+                g_value,
+                g_bvalue,
+                g_out,
+                g_bout,
+                g_gain_two,
+                g_shift_two,
+                g_up,
+                g_bup,
+                g_down,
+                g_bdown,
+            ),
+            "seq",
         ),
-        ("dp", "seq"),
+        "dp",
     )
     return (
         output,

time: 919 us -> 1340 us (1.46)
  waiting for transfers between devices: 367 us -> 743 us
  blocking collectives: 59.1 us -> 99.5 us
    psum x0 -> x1, waiting for transfers between devices: none -> 649 us  [local(): lax.psum(lax.psum((g_gain_one, g_shift_one, g_query, g_bquery, g_key, g_v...]
    psum x1, waiting for transfers between devices: 367 us -> 94.4 us  [local(): lax.psum((g_gain_one, g_shift_one, g_query, g_bquery, g_key, g_value, g_b...]
    psum x0 -> x1, blocking collectives: none -> 82.6 us  [local(): lax.psum(lax.psum((g_gain_one, g_shift_one, g_query, g_bquery, g_key, g_v...]
    psum x1, blocking collectives: 45.7 us -> 3.6 us  [local(): lax.psum((g_gain_one, g_shift_one, g_query, g_bquery, g_key, g_value, g_b...]
  transfers between devices with their start and end apart: 7 -> 8, of which waited for: 1 -> 2; matrix products, arithmetic and copies ran while one was open for 11% -> 8% of each run, Pallas kernels for 0% -> 0%
where the time goes in v1:
time: 1340 us; the launch traced here: 1330 us
  waiting for transfers between devices  743 us (55%)
  matrix products  192 us (14%)
  local copies, waits for them, and re-layouts  174 us (13%)
  blocking collectives  99.5 us (7%)
  other arithmetic  71.9 us (5%)
  starting transfers between devices  29.5 us (2%)
  between operations  14.9 us (1%)
    psum x1, waiting for transfers between devices, local(): lax.psum(lax.psum((g_gain_one, g_shift_one, g_query, g_bquery, g_key, g_v...  649 us
    psum x1, waiting for transfers between devices, local(): lax.psum((g_gain_one, g_shift_one, g_query, g_bquery, g_key, g_value, g_b...  94.4 us
    psum x1, blocking collectives, local(): lax.psum(lax.psum((g_gain_one, g_shift_one, g_query, g_bquery, g_key, g_v...  82.6 us
    dot_general x6, matrix products, project_back(): jnp.einsum('stf,df->std', grad_rows, weight, preferred_element_type=jnp.f...  42.1 us
    dot_general x6, matrix products, weight_grad(): jnp.einsum('std,stf->df', left_rows, grad_rows, preferred_element_type=jn...  37.4 us
    dot_general x6, matrix products, project(): return jnp.dot(left_rows, weight, preferred_element_type=jnp.float32)  34.7 us
    convert_element_type x1, other arithmetic, local(): active = exact_gelu(upper_pre).astype(jnp.bfloat16)  32.4 us
    dynamic_slice x36, local copies, waits for them, and re-layouts, local(): lax.map(attend, (query_whole, key_whole, value_whole, lengths))  32.2 us
  transfers between devices with their start and end apart: 8, of which 2 were waited for; matrix products, arithmetic and copies ran while one was open for 8% of the time, Pallas kernels for 0%

profile of v1, /device:TPU:0, one launch (start us, length us, event | category | flops | bytes accessed | tf_op | source)
XLA Modules:
  0.0 1325.9 jit_solution(5285887293343845159)
XLA Ops:
  11.3 2.9 add_convert_fusion.4
  14.2 5.1 copy.101
  19.4 5.1 all-to-all-start
  24.5 4.2 add_convert_fusion.3
  28.7 5.1 copy.104
  33.8 4.9 all-to-all-start.1
  38.8 7.2 copy.136
  46.0 2.8 copy.103
  48.8 3.8 copy.110
  52.6 4.2 convolution_convert_fusion.1
  56.8 5.1 copy.107
  62.0 5.5 all-to-all-start.2
  67.4 7.2 copy.137
  74.6 2.8 copy.106
  77.4 3.8 copy.111
  81.3 7.2 copy.138
  88.4 2.8 copy.109
  91.3 3.8 copy.112
  96.5 45.2 %while.26 = (s32[]{:T(128)}, bf16[4,544,384]{1,2,0:T(8,128)(2,1)}, f32[4,6,544]{2,1,0:T(8,128)}, bf16[4,544,384]{1,2,0:T(8,128)(2,1)}, s32[4]{0:T(128)S(1)}, /*i...) while((s32[]{:T(128)}, bf16[4,544,384]{1,2,0:T(8,128)(2,1)}, ...), condition=%wide.region_5.6_spmd, body=%wide.region_2.5_spmd.sunk | while | flops 476071264 | bytes 26508796 | solution.py:140
  141.8 4.7 copy.113
  146.5 6.4 all_to_all.144
  156.7 11.9 fusion.47
  168.6 32.4 %multiply_convert_fusion.1 = (bf16[4,272,3072]{2,1,0:T(8,128)(2,1)}, f32[4,272,3072]{2,1,0:T(8,128)}) fusion(f32[4,272,3072]{2,1,0:T(8,128)S(1)} %get-tuple-element.254, f32[3072]{0:T(1024)S(1)} %copy-done.30, u8[272,3072]{1,0:T(8,128)(4,1)S(1)} %get-tuple-element.166, u8[272,3072]{1,0:T(8,128)(4,1)S(1)} %get-tuple-element.165), kind=kLoop, calls=%fused_computation.46 | loop fusion | flops 237305856 | bytes 35106816 | tf_op jit(solution)/shard_map/convert_element_type | solution.py:145
  200.9 19.9 %convert_reduce_fusion = (f32[3072]{0:T(1024)}, bf16[4,272,3072]{2,1,0:T(8,128)(2,1)}) fusion(f32[4,272,3072]{2,1,0:T(8,128)} %get-tuple-element.242, bf16[4,272,768]{2,1,0:T(8,128)(2,1)} %param.39, bf16[3072,768]{1,0:T(8,128)(2,1)} %param.37, f32[4,272,3072]{2,1,0:T(8,128)} %copy-done.9, f32[3072]{0:T(1024)S(1)} %copy-done.30), kind=kOutput, calls=%fused_computation.44 | convolution fusion | flops 5190644736 | bytes 39837696 | tf_op jit(solution)/shard_map/stf,df->std/dot_general | solution.py:19
  220.9 10.6 multiply_reduce_fusion.1
  235.5 2.7 convolution_convert_fusion
  238.2 3.9 copy.116
  242.1 6.9 all_to_all.145
  249.0 7.0 copy.139
  261.8 105.1 %while.27 = (s32[]{:T(128)}, bf16[4,544,384]{1,2,0:T(8,128)(2,1)}, bf16[4,544,384]{1,2,0:T(8,128)(2,1)}, bf16[4,544,384]{1,2,0:T(8,128)(2,1)}, bf16[4,544,384]{1...) while((s32[]{:T(128)}, bf16[4,544,384]{1,2,0:T(8,128)(2,1)}, ...), condition=%wide.region_12.13_spmd, body=%wide.region_10.12_spmd.sunk | while | flops 1164070272 | bytes 89513552 | solution.py:167
  263.9 4.7 fusion.133
  273.0 6.1 multiply_reduce_fusion.7
  279.1 2.6 multiply_convert_fusion.3
  290.2 4.7 fusion.133
  299.3 6.1 multiply_reduce_fusion.7
  305.4 2.6 multiply_convert_fusion.3
  316.4 4.7 fusion.133
  325.5 6.1 multiply_reduce_fusion.7
  342.7 4.7 fusion.133
  351.8 6.1 multiply_reduce_fusion.7
  357.9 2.6 multiply_convert_fusion.3
  366.9 4.8 copy.129
  371.7 4.7 all-to-all-start.7
  376.4 5.2 convolution_bitcast_fusion.2
  381.6 12.3 convolution_bitcast_fusion.1
  394.0 3.0 copy.123
  396.9 4.7 all-to-all-start.5
  404.6 4.7 copy.126
  409.3 4.7 all-to-all-start.6
  420.7 3.6 convolution_bitcast_fusion.5
  424.3 3.6 convolution_bitcast_fusion.4
  427.9 3.6 convolution_bitcast_fusion.3
  431.5 9.1 convolution_bitcast_fusion
  440.6 94.4 %all-reduce.9.cloned.1.call-done = (f32[768,768]{1,0:T(8,128)}, f32[768,768]{1,0:T(8,128)}, f32[768,768]{1,0:T(8,128)}, f32[768,768]{1,0:T(8,128)}, f32[768,3072]{1,0:T(8,128)}, /*index=5*/f32[3072,768]{1,0:T(8,128)}) async-done(((f32[768,768]{1,0:T(8,128)}, f32[768,768]{1,0:T(8,128)}, f32[768,768]{1,0:T(8,128)}, f32[768,768]{1,0:T(8,128)}, f32[768,3072]{1,0:T(8,128)}, /*index=5*/f32[3072,768]{1,0:T(8,128)}), ...) | async-done | bytes 28311568 | tf_op jit(solution)/shard_map/psum | solution.py:206
  537.2 3.4 fusion.55
  542.6 3.9 fusion.43
  546.5 3.6 all-reduce.2
  550.2 82.6 %all-reduce = (f32[768]{0:T(1024)}, f32[768]{0:T(1024)}, f32[768]{0:T(1024)}, f32[768]{0:T(1024)}, f32[768]{0:T(1024)}, /*index=5*/f32[768]{0:T(1024)}, f32[768]{0:T(1024)}, f32[3072]{0:T(1024)}, f32[768]{0:T(1024)}) all-reduce(f32[768]{0:T(1024)S(1)} %get-tuple-element.224, ...), channel_id=1, replica_groups=mesh['dp'=16,'seq'=2] {'dp'}, use_global_device_ids=true, to_apply=%region_17.18 | all-reduce | flops 9216 | bytes 73728 | tf_op jit(solution)/shard_map/psum | solution.py:205
  632.7 4.7 fusion.42
  637.4 9.8 add_convert_fusion.1
  647.2 648.6 %all-reduce.7.cloned.1.call-done = (f32[768,768]{1,0:T(8,128)}, f32[768,768]{1,0:T(8,128)}, f32[768,768]{1,0:T(8,128)}, f32[768,768]{1,0:T(8,128)}, f32[768,3072]{1,0:T(8,128)}, /*index=5*/f32[3072,768]{1,0:T(8,128)}) async-done(((f32[768,768]{1,0:T(8,128)}, f32[768,768]{1,0:T(8,128)}, f32[768,768]{1,0:T(8,128)}, f32[768,768]{1,0:T(8,128)}, f32[768,3072]{1,0:T(8,128)}, /*index=5*/f32[3072,768]{1,0:T(8,128)}), ...) | async-done | bytes 28311568 | tf_op jit(solution)/shard_map/psum | solution.py:205
  1295.9 3.4 copy.187
  1305.7 9.3 copy.191
  1315.0 3.7 copy.192
  (267 shorter events, 138.3 us)
Async XLA Ops:
  7.2 4.1 copy-start
  7.2 4.1 copy-start.2
  7.2 4.0 copy-start.41
  7.2 4.0 copy-start.46
  7.2 4.0 copy-start.34
  9.2 43.5 %copy-start.24 = (f32[4,272]{1,0:T(4,128)}, f32[4,272]{1,0:T(4,128)S(1)}, u32[]{:S(2)}) copy-start(f32[4,272]{1,0:T(4,128)S(1)} %broadcast_multiply_fusion.5) | copy-start | bytes 13060
  11.3 41.3 %copy-start.26 = (f32[4,272]{1,0:T(4,128)}, f32[4,272]{1,0:T(4,128)S(1)}, u32[]{:S(2)}) copy-start(f32[4,272]{1,0:T(4,128)S(1)} %add_rsqrt_fusion.1) | copy-start | bytes 13060
  19.4 5.1 copy-start.42
  19.4 14.5 %all-to-all-start = ((bf16[4,272,768]{1,0,2:T(4,128)(2,1)}), bf16[4,272,768]{1,0,2:T(4,128)(2,1)}, u32[]{:S(2)}, u32[]{:S(2)}) async-start(bf16[4,272,768]{1,0,2:T(4,128)(2,1)} %copy.101), calls=%async_computation | async-start | bytes 4718592 | tf_op jit(solution)/shard_map/all_to_all | solution.py:138
  33.8 28.1 %all-to-all-start.1 = ((bf16[4,272,768]{1,0,2:T(4,128)(2,1)}), bf16[4,272,768]{1,0,2:T(4,128)(2,1)}, u32[]{:S(2)}, u32[]{:S(2)}) async-start(bf16[4,272,768]{1,0,2:T(4,128)(2,1)} %copy.104), calls=%async_computation.1 | async-start | bytes 4718592 | tf_op jit(solution)/shard_map/all_to_all | solution.py:136
  62.0 19.3 %all-to-all-start.2 = ((bf16[4,272,768]{1,0,2:T(4,128)(2,1)}), bf16[4,272,768]{1,0,2:T(4,128)(2,1)}, u32[]{:S(2)}, u32[]{:S(2)}) async-start(bf16[4,272,768]{1,0,2:T(4,128)(2,1)} %copy.107), calls=%async_computation.2 | async-start | bytes 4718592 | tf_op jit(solution)/shard_map/all_to_all | solution.py:137
  91.3 5.3 copy-start.49
  153.3 2.6 copy-start.15
  155.8 12.7 copy-start.5
  168.5 32.4 %copy-start.9 = (f32[4,272,3072]{2,1,0:T(8,128)}, f32[4,272,3072]{2,1,0:T(8,128)S(1)}, u32[]{:S(2)}) copy-start(f32[4,272,3072]{2,1,0:T(8,128)S(1)} %get-tuple-element.254) | copy-start | bytes 40108036
  200.9 19.9 %copy-start.6 = (f32[4,272,768]{2,1,0:T(8,128)S(1)}, f32[4,272,768]{2,1,0:T(8,128)}, u32[]{:S(2)}) copy-start(f32[4,272,768]{2,1,0:T(8,128)} %copy-done.5) | copy-start | bytes 10027012
  220.9 10.6 copy-start.22
  231.5 4.0 copy-start.39
  257.4 4.3 copy-start.50
  273.0 6.1 slice-start
  273.0 6.1 slice-start.1
  299.2 6.1 slice-start
  299.3 6.1 slice-start.1
  325.5 6.1 slice-start
  325.5 6.1 slice-start.1
  351.8 6.1 slice-start
  351.8 6.1 slice-start.1
  366.9 9.5 copy-start.16
  371.7 25.3 %all-to-all-start.7 = ((bf16[4,544,384]{2,0,1:T(4,128)(2,1)}), bf16[4,544,384]{2,0,1:T(4,128)(2,1)}, u32[]{:S(2)}, u32[]{:S(2)}) async-start(bf16[4,544,384]{2,0,1:T(4,128)(2,1)} %copy.129), calls=%async_computation.7 | async-start | bytes 3342336 | tf_op jit(solution)/shard_map/all_to_all | solution.py:173
  376.3 5.3 copy-start.7
  376.3 5.3 copy-start.33
  376.4 5.3 copy-start.45
  381.6 12.3 copy-start.11
  396.9 12.3 all-to-all-start.5
  409.3 8.9 all-to-all-start.6
  414.0 121.1 %all-reduce.9.cloned.1.call-start = ((), (), s32[]{:S(2)}) async-start(), calls=%async_computation.9 | async-start | bytes 56623104 | tf_op jit(solution)/shard_map/psum | solution.py:206
  418.2 2.0 copy-start.25
  418.2 2.1 copy-start.27
  418.2 2.1 copy-start.35
  418.2 2.1 copy-start.47
  418.2 2.1 copy-start.3
  418.2 2.5 copy-start.19
  420.2 4.0 copy-start.20
  424.3 3.6 copy-start.17
  424.3 7.1 slice-start.5
  427.9 3.6 slice-start.6
  427.9 3.6 copy-start.23
  440.6 855.3 %all-reduce.7.cloned.1.call-start = ((), (), s32[]{:S(2)}) async-start(), calls=%async_computation.8 | async-start | bytes 56623104 | tf_op jit(solution)/shard_map/psum | solution.py:205
  537.2 3.5 copy-start.21
  537.2 3.5 copy-start.40
  540.6 1.9 copy-start.18
  542.6 3.9 copy-start.28
  542.6 3.9 copy-start.29
  542.6 3.9 copy-start.31
  542.6 3.9 copy-start.36
  542.6 3.9 copy-start.37
  632.7 4.7 copy-start.8
  632.7 4.7 copy-start.48
  1295.9 3.4 copy-start.14
  1299.3 2.5 copy-start.13
  1301.8 2.5 copy-start.12
  1304.3 10.7 slice-start.2
  1305.7 9.3 slice-start.3
  1305.7 9.3 slice-start.4
  (8 other events, 9.3 us)
Sparse Core Ops, SparseCore 0:
  440.7 94.3 all-reduce.8
  541.5 754.3 all-reduce.6
